TPU v7x, 32 devices: a whole 2x2x4 slice. The times are simulated.
32 devices in a mesh: run: 2 (over y), lon: 4 (over z), node: 2 (over x), lev: 2 (over core).
Axes of the slice: x: 2, y: 2, z: 4, core: 2. Of those that a mesh axis runs over, the one named last changes fastest.
Arguments:
- initial_state: float32 [8, 4, 96, 512], P(None, 'lev', 'run', 'lon'), parts along dimension 2, may hold values from -6 to 6
- node_states: float32 [8, 8, 4, 96, 512], P('node', None, 'lev', 'run', 'lon'), parts along dimension 3, may hold values from -6 to 6
- node_order: int32 [8], replicated, may hold values from 0 to 7, each once
- sector_depth: int32 [8, 96], P('node', 'run'), parts along dimension 1, may hold values from 0 to 2, as said below
- cell_offset: int32 [8, 96], P('node', 'run'), parts along dimension 1, may hold values from 2 to 127
- fraction: float32 [8, 96], P('node', 'run'), parts along dimension 1, may hold values from 0 to 1
- reaction_matrix: float32 [8, 8], replicated, may hold values from -2 to 2
- diffusivity: float32 [4], P('lev'), may hold values from 0.1 to 1
Outputs:
- new_states: float32 [8, 8, 4, 96, 512], P('node', None, 'lev', 'run', 'lon'), parts along dimension 3
There are 2 independent parts, one for each index of `run`. A program takes and returns all parts, laid end to end along the dimension named above; an argument that names none is the same for every part. Nothing has to cross between parts.
Inputs may be any that keep to these rules, and one draw needn't show every extreme that they name: `sector_depth`: rows among the 6 nearest either pole have depth 2 or more, all other rows depth 0 or 1; the rows at both poles have depth 2, the middle row depth 0.
All inputs are finite; a program needn't handle non-finite values.
Results may differ from a plain program's by a relative error of at most 0.0003.
Values sent between devices are 32-bit elements; how exact they have to be, the bound alone decides.
A program may use at most 128 MiB of HBM per device.

v0:
```python
import jax
import jax.numpy as jnp
import numpy as np
from jax import lax
from jax.sharding import PartitionSpec as P

NODES = 8
time_step = 0.5
lobatto_points = [
    -1.0,
    -0.8717401485096066,
    -0.5917001814331423,
    -0.2092992179024789,
    0.2092992179024789,
    0.5917001814331423,
    0.8717401485096066,
    1.0,
]


def padded_2(array, sides, width):
    for axis, dim in sides:
        size, length = (lax.axis_size(axis), array.shape[dim])
        up = [(i, (i + 1) % size) for i in range(size - 1)]
        down = [(j, i) for i, j in up]
        last = lax.slice_in_dim(array, length - width, length, axis=dim)
        first = lax.slice_in_dim(array, 0, width, axis=dim)
        before = lax.ppermute(last, axis, up)
        after = lax.ppermute(first, axis, down)
        array = jnp.concatenate([before, array, after], axis=dim)
    return array


def passed_along(array, axis, by):
    length = lax.axis_size(axis)
    return lax.ppermute(array, axis, [(i, (i + by) % length) for i in range(length)])


def lobatto_table():
    points = [(value + 1.0) / 2.0 for value in lobatto_points]
    result_rows = [[0.0] * 8 for m in range(8)]
    for j in range(8):
        poly_coeffs = [1.0]
        for k in range(8):
            if k != j:
                factor = 1.0 / (points[j] - points[k])
                grown = [0.0] * (len(poly_coeffs) + 1)
                for i in range(len(poly_coeffs)):
                    grown[i + 1] = grown[i + 1] + poly_coeffs[i] * factor
                    grown[i] = grown[i] - poly_coeffs[i] * points[k] * factor
                poly_coeffs = grown
        for m in range(8):
            total_value = 0.0
            for i in range(len(poly_coeffs)):
                total_value = total_value + poly_coeffs[i] * points[m] ** (i + 1) / (i + 1)
            result_rows[m][j] = total_value
    return np.array(result_rows)


def cubic_weights(fraction):
    return (
        -fraction * (fraction - 1.0) * (fraction - 2.0) / 6.0,
        (fraction + 1.0) * (fraction - 1.0) * (fraction - 2.0) / 2.0,
        -(fraction + 1.0) * fraction * (fraction - 2.0) / 2.0,
        (fraction + 1.0) * fraction * (fraction - 1.0) / 6.0,
    )


def section_matrix(node_order):
    onehot = (node_order[:, None] == jnp.arange(NODES, dtype=jnp.int32)[None, :]).astype(
        jnp.float32
    )
    quad_values = jnp.asarray(lobatto_table(), jnp.float32)
    left = jnp.dot(onehot, quad_values, precision=lax.Precision.HIGHEST)
    return jnp.dot(left, onehot.T, precision=lax.Precision.HIGHEST)


def tendency_of(states, reaction_matrix, diffusivity):
    level_count = states.shape[2]
    padded = padded_2(states, (("lev", 2),), 1)
    level_pos = lax.axis_index("lev")
    level_last = lax.axis_size("lev") - 1
    below = padded[:, :, :level_count]
    above = padded[:, :, 2:]
    bottom_level = jnp.where(level_pos == 0, states[:, :, :1], below[:, :, :1])
    below = jnp.concatenate([bottom_level, below[:, :, 1:]], axis=2)
    top_level = jnp.where(
        level_pos == level_last, states[:, :, level_count - 1 :], above[:, :, level_count - 1 :]
    )
    above = jnp.concatenate([above[:, :, : level_count - 1], top_level], axis=2)
    curvature = above - 2.0 * states + below
    reaction = jnp.einsum(
        "ts,mslyx->mtlyx", reaction_matrix, jnp.tanh(states), precision=lax.Precision.HIGHEST
    )
    return reaction + diffusivity[None, None, :, None, None] * curvature


def cut_window(field, start, length):
    return lax.dynamic_slice_in_dim(field, start, length, 2)


def advect_rows(sectioned, sector_depth, cell_offset, fraction):
    sector_cells = sectioned.shape[4]
    reach_max = min(4, lax.axis_size("lon") - 2) + 1
    depth_cells = sector_depth[:, None, None, :, None]
    nearer = jnp.where(depth_cells == 0, sectioned, 0.0)
    farther = jnp.zeros_like(sectioned)
    previous = sectioned
    for distance in range(1, reach_max + 1):
        source = previous
        arrived = passed_along(source, "lon", 1)
        previous = arrived
        nearer = nearer + jnp.where(depth_cells == distance, arrived, 0.0)
        farther = farther + jnp.where(depth_cells + 1 == distance, arrived, 0.0)
    window = jnp.concatenate([farther, nearer], axis=4)
    starts = sector_cells - cell_offset - 1
    cut_len = sector_cells + 3
    per_row = jax.vmap(cut_window, in_axes=(2, 0, None), out_axes=2)
    per_slot = jax.vmap(per_row, in_axes=(0, 0, None), out_axes=0)
    pieces = per_slot(window, starts, cut_len)
    coeffs = cubic_weights(fraction)
    result = jnp.zeros_like(sectioned)
    for stencil in range(4):
        result = (
            result
            + coeffs[stencil][:, None, None, :, None]
            * pieces[:, :, :, :, stencil : stencil + sector_cells]
        )
    return result


def shards(
    initial_state,
    node_states,
    node_order,
    sector_depth,
    cell_offset,
    fraction,
    reaction_matrix,
    diffusivity,
):
    slots = node_states.shape[0]
    weights = section_matrix(node_order)
    node_pos = lax.axis_index("node")
    tendency = tendency_of(node_states, reaction_matrix, diffusivity)
    own_rows = lax.dynamic_slice_in_dim(weights, node_pos * slots, slots, 0)
    integral = jnp.einsum(
        "mj,jtlyx->mtlyx",
        own_rows,
        lax.all_gather(tendency, "node", axis=0, tiled=True),
        precision=lax.Precision.HIGHEST,
    )
    sectioned = initial_state[None] + time_step * integral
    return advect_rows(sectioned, sector_depth, cell_offset, fraction)


def solution(mesh):
    in_specs = (
        P(None, "lev", "run", "lon"),
        P("node", None, "lev", "run", "lon"),
        P(),
        P("node", "run"),
        P("node", "run"),
        P("node", "run"),
        P(),
        P("lev"),
    )
    out_specs = P("node", None, "lev", "run", "lon")
    return jax.shard_map(shards, mesh=mesh, in_specs=in_specs, out_specs=out_specs, check_vma=False)
```

profile of v0, /device:TPU:0, one launch (start us, length us, event | category | flops | bytes accessed | tf_op | source)
XLA Modules:
  0.0 328.9 jit_solution(18254070785637578791)
XLA Ops:
  6.5 0.0 copy-start
  6.5 0.0 all-gather.2.cloned.1.call-start
  6.5 2.8 fusion.31
  9.3 1.3 collective-permute-start
  10.6 4.8 %collective-permute-start.1 = (f32[4,8,1,48,128]{4,3,2,1,0:T(8,128)}, f32[4,8,1,48,128]{4,3,2,1,0:T(8,128)}, u32[]{:S(2)}, u32[]{:S(2)}) collective-permute-start(f32[4,8,1,48,128]{4,3,2,1,0:T(8,128)} %get-tuple-element.9), channel_id=1, source_target_pairs={{0,1},{2,3},{4,5},{6,7},{8,9},{10,11},{12,13},{14,15},{16,17},{18,... | collective-permute-start | bytes 2359304 | tf_op jit(solution)/shard_map/ppermute | solution.py:28
  15.4 0.0 copy-done.2
  15.4 0.2 tanh.3
  15.6 0.0 copy-done
  15.6 2.4 fusion.8
  18.1 0.0 copy-start.7
  18.1 0.0 collective-permute-done
  18.1 0.0 collective-permute-done.1
  18.1 1.4 broadcast_select_fusion
  19.5 0.0 copy-done.7
  19.5 3.2 fusion.7
  22.7 0.0 all-gather.2.cloned.1.call-update
  22.7 0.6 copy-done.8
  23.4 0.0 copy-done.9
  23.4 0.2 fusion.14
  23.6 0.2 fusion.13
  23.8 0.0 copy-start.4
  23.8 46.7 %all-gather.2.cloned.1.call-done = f32[8,8,2,48,128]{4,3,2,1,0:T(8,128)} async-done(((f32[4,8,2,48,128]{4,3,2,1,0:T(8,128)}), f32[8,8,2,48,128]{4,3,2,1,0:T(8,128)}) %all-gather.2.cloned.1.call-update) | async-done | bytes 3145744 | tf_op jit(solution)/shard_map/all_gather | solution.py:150
  70.5 0.0 copy-done.3
  70.5 6.5 %multiply_add_fusion = f32[4,8,2,48,128]{4,0,3,2,1:T(4,128)S(1)} fusion(f32[8,8,2,48,128]{4,3,2,1,0:T(8,128)} %all-gather.2.cloned.1.call-done, f32[8,2,48,128]{3,2,1,0:T(8,128)S(1)} %copy-done.3, f32[8,8]{1,0:T(8,128)S(1)} %fusion.13, s32[]{:T(128)S(6)} %select_n.42), kind=kOutput, calls=%fused_computation.19 | convolution fusion | flops 38535168 | bytes 5113860 | tf_op jit(solution)/shard_map/mj,jtlyx->mtlyx/dot_general | solution.py:147
  77.0 1.5 collective-permute-start.2
  78.6 36.4 %collective-permute-done.2 = f32[4,8,2,48,128]{4,0,3,2,1:T(4,128)S(1)} collective-permute-done((f32[4,8,2,48,128]{4,0,3,2,1:T(4,128)S(1)}, f32[4,8,2,48,128]{4,0,3,2,1:T(4,128)S(1)}, u32[]{:S(2)}, u32[]{:S(2)}) %collective-permute-start.2) | collective-permute-done | bytes 1572896 | tf_op jit(solution)/shard_map/ppermute | solution.py:36
  115.0 0.0 collective-permute-start.3
  115.0 37.2 %collective-permute-done.3 = f32[4,8,2,48,128]{4,0,3,2,1:T(4,128)} collective-permute-done((f32[4,8,2,48,128]{4,0,3,2,1:T(4,128)S(1)}, f32[4,8,2,48,128]{4,0,3,2,1:T(4,128)}, u32[]{:S(2)}, u32[]{:S(2)}) %collective-permute-start.3) | collective-permute-done | bytes 1572896 | tf_op jit(solution)/shard_map/ppermute | solution.py:36
  152.2 0.0 collective-permute-start.4
  152.2 0.0 copy-done.6
  152.2 0.1 copy.22
  152.3 0.1 copy.24
  152.4 0.1 copy.25
  152.5 0.1 copy.26
  152.7 0.1 copy.27
  152.8 0.1 copy.28
  152.9 0.1 copy.29
  153.0 0.0 copy-done.5
  153.0 0.1 reshape.22
  153.1 0.0 copy-done.4
  153.1 35.6 %collective-permute-done.4 = f32[4,8,2,48,128]{4,0,3,2,1:T(4,128)} collective-permute-done((f32[4,8,2,48,128]{4,0,3,2,1:T(4,128)}, f32[4,8,2,48,128]{4,0,3,2,1:T(4,128)}, u32[]{:S(2)}, u32[]{:S(2)}) %collective-permute-start.4) | collective-permute-done | bytes 1572896 | tf_op jit(solution)/shard_map/ppermute | solution.py:36
  188.6 3.9 %select_add_fusion.1 = (f32[4,8,2,48,128]{4,0,3,2,1:T(4,128)S(1)}, f32[4,8,2,48,128]{4,0,3,2,1:T(4,128)S(1)}) fusion(f32[4,8,2,48,128]{4,0,3,2,1:T(4,128)} %collective-permute-done.4, f32[4,8,2,48,128]{4,0,3,2,1:T(4,128)} %collective-permute-done.3, f32[4,8,2,48,128]{4,0,3,2,1:T(4,128)S(1)} %collective-permute-done.2, pred[4,48]{0,1:T(8,128)(4,1)S(1)} %copy.25, ...), kind=kLoop, calls=%fused_computation.18 | loop fusion | flops 4718592 | bytes 9438528 | tf_op jit(solution)/shard_map/add | solution.py:114
  192.5 0.8 maximum_bitcast_fusion
  193.3 52.7 %copy.30 = f32[4,48,8,2,256]{2,3,1,0,4:T(2,128)} copy(f32[4,48,8,2,256]{4,0,1,3,2:T(4,128)S(1)} %maximum_bitcast_fusion) | data formatting | bytes 6291456 | tf_op jit(solution)/shard_map/vmap(vmap())/transpose | solution.py:99
  246.0 36.2 %gather_fusion = f32[192,8,2,131]{1,2,3,0:T(2,128)} fusion(f32[4,48,8,2,256]{2,3,1,0,4:T(2,128)} %copy.30, s32[192]{0:T(256)S(1)} %reshape.22), kind=kCustom, calls=%fused_computation | custom fusion | bytes 3223296 | tf_op jit(solution)/shard_map/vmap(vmap())/gather | solution.py:99
  282.2 37.2 %copy.31 = f32[4,48,8,2,131]{4,1,3,2,0:T(8,128)S(1)} copy(f32[4,48,8,2,131]{2,3,4,1,0:T(2,128)} %bitcast.24) | data formatting | bytes 3219456 | tf_op jit(solution)/shard_map/vmap(vmap())/gather | solution.py:99
  319.4 0.0 copy-start.1
  319.5 2.5 fusion.2
  (10 shorter events, 0.0 us)
Async XLA Ops:
  6.5 9.1 %copy-start = (f32[8,8]{1,0:T(8,128)S(1)}, f32[8,8]{1,0:T(8,128)}, u32[]{:S(2)}) copy-start(f32[8,8]{1,0:T(8,128)} %param.15) | copy-start | bytes 772
  6.5 8.9 %copy-start.2 = (f32[4,8,2,48,128]{4,3,2,1,0:T(8,128)S(1)}, f32[4,8,2,48,128]{4,3,2,1,0:T(8,128)}, u32[]{:S(2)}) copy-start(f32[4,8,2,48,128]{4,3,2,1,0:T(8,128)} %param.10) | copy-start | bytes 4718596
  6.5 64.0 %all-gather.2.cloned.1.call-start = ((), (), s32[]{:S(2)}) async-start(), calls=%async_computation | async-start | bytes 4718592 | tf_op jit(solution)/shard_map/all_gather | solution.py:150
  9.3 8.8 %collective-permute-start = (f32[4,8,1,48,128]{4,3,2,1,0:T(8,128)}, f32[4,8,1,48,128]{4,3,2,1,0:T(8,128)}, u32[]{:S(2)}, u32[]{:S(2)}) collective-permute-start(f32[4,8,1,48,128]{4,3,2,1,0:T(8,128)} %get-tuple-element.10), channel_id=1, source_target_pairs={{1,0},{3,2},{5,4},{7,6},{9,8},{11,10},{13,12},{15,14},{17,16},{19,... | collective-permute-start | bytes 2359304 | tf_op jit(solution)/shard_map/ppermute | solution.py:29
  10.6 7.5 %collective-permute-start.1 = (f32[4,8,1,48,128]{4,3,2,1,0:T(8,128)}, f32[4,8,1,48,128]{4,3,2,1,0:T(8,128)}, u32[]{:S(2)}, u32[]{:S(2)}) collective-permute-start(f32[4,8,1,48,128]{4,3,2,1,0:T(8,128)} %get-tuple-element.9), channel_id=1, source_target_pairs={{0,1},{2,3},{4,5},{6,7},{8,9},{10,11},{12,13},{14,15},{16,17},{18,... | collective-permute-start | bytes 2359304 | tf_op jit(solution)/shard_map/ppermute | solution.py:28
  18.1 1.5 copy-start.7
  22.7 0.7 copy-start.8
  22.7 0.7 copy-start.9
  22.7 47.8 %copy-start.3 = (f32[8,2,48,128]{3,2,1,0:T(8,128)S(1)}, f32[8,2,48,128]{3,2,1,0:T(8,128)}, u32[]{:S(2)}) copy-start(f32[8,2,48,128]{3,2,1,0:T(8,128)} %param.9) | copy-start | bytes 1179652
  23.8 128.4 %copy-start.6 = (s32[4,48]{1,0:T(4,128)S(1)}, s32[4,48]{1,0:T(4,128)}, u32[]{:S(2)}) copy-start(s32[4,48]{1,0:T(4,128)} %param.12) | copy-start | bytes 2308
  23.8 129.2 %copy-start.5 = (s32[4,48]{1,0:T(4,128)S(1)}, s32[4,48]{1,0:T(4,128)}, u32[]{:S(2)}) copy-start(s32[4,48]{1,0:T(4,128)} %param.13) | copy-start | bytes 2308
  23.8 129.3 %copy-start.4 = (f32[4,48]{1,0:T(4,128)S(1)}, f32[4,48]{1,0:T(4,128)}, u32[]{:S(2)}) copy-start(f32[4,48]{1,0:T(4,128)} %param.14) | copy-start | bytes 2308
  77.0 38.0 %collective-permute-start.2 = (f32[4,8,2,48,128]{4,0,3,2,1:T(4,128)S(1)}, f32[4,8,2,48,128]{4,0,3,2,1:T(4,128)S(1)}, u32[]{:S(2)}, u32[]{:S(2)}) collective-permute-start(f32[4,8,2,48,128]{4,0,3,2,1:T(4,128)S(1)} %multiply_add_fusion), channel_id=1, source_target_pairs={{0,4},{4,8},{8,12},{12,0},{1,5},{5,9},{9,13},{13,1},{2,6},{6,10},{... | collective-permute-start | bytes 4718600 | tf_op jit(solution)/shard_map/ppermute | solution.py:36
  115.0 37.2 %collective-permute-start.3 = (f32[4,8,2,48,128]{4,0,3,2,1:T(4,128)S(1)}, f32[4,8,2,48,128]{4,0,3,2,1:T(4,128)}, u32[]{:S(2)}, u32[]{:S(2)}) collective-permute-start(f32[4,8,2,48,128]{4,0,3,2,1:T(4,128)S(1)} %collective-permute-done.2), channel_id=1, source_target_pairs={{0,4},{4,8},{8,12},{12,0},{1,5},{5,9},{9,13},{13,1},{2,6},{6,10},{... | collective-permute-start | bytes 4718600 | tf_op jit(solution)/shard_map/ppermute | solution.py:36
  152.2 36.5 %collective-permute-start.4 = (f32[4,8,2,48,128]{4,0,3,2,1:T(4,128)}, f32[4,8,2,48,128]{4,0,3,2,1:T(4,128)}, u32[]{:S(2)}, u32[]{:S(2)}) collective-permute-start(f32[4,8,2,48,128]{4,0,3,2,1:T(4,128)} %collective-permute-done.3), channel_id=1, source_target_pairs={{0,4},{4,8},{8,12},{12,0},{1,5},{5,9},{9,13},{13,1},{2,6},{6,10},{... | collective-permute-start | bytes 4718600 | tf_op jit(solution)/shard_map/ppermute | solution.py:36
  319.4 2.6 copy-start.1
Sparse Core Ops, SparseCore 0:
  22.8 47.6 all-gather.1
where the time goes:
time: 330 us; the launch traced here: 329 us
  waiting for transfers between devices  156 us (47%)
  local copies, waits for them, and re-layouts  131 us (40%)
  between operations  13.5 us (4%)
  other arithmetic  11.8 us (4%)
  matrix products  9.28 us (3%)
  starting transfers between devices  7.63 us (2%)
    ppermute x3, waiting for transfers between devices, passed_along(): lax.ppermute(array, axis, [(i, (i + by) % length) for i in range(length)])  109 us
    gather x3, local copies, waits for them, and re-layouts, cut_window(): return lax.dynamic_slice_in_dim(field, start, length, 2)  73.5 us
    transpose x1, local copies, waits for them, and re-layouts, cut_window(): return lax.dynamic_slice_in_dim(field, start, length, 2)  52.7 us
    all_gather x1, waiting for transfers between devices, shards(): lax.all_gather(tendency, 'node', axis=0, tiled=True)  46.7 us
  transfers between devices with their start and end apart: 6, of which 4 were waited for; matrix products, arithmetic and copies ran while one was open for 1% of the time, Pallas kernels for 0%

commit v1 on v0

--- a/solution.py
+++ b/solution.py
@@ -16,6 +16,23 @@
     0.8717401485096066,
     1.0,
 ]
+
+
+def group_the_levels_all(x0, peer_axis, point):
+    arr_now = jax.lax.axis_size(peer_axis)
+    block_last = jax.lax.axis_index(peer_axis)
+    vec_out, oldest = (arr_now, block_last)
+    bank = [(jj, (jj - 1) % vec_out) for jj in range(vec_out)]
+    z_new = x0
+    taken_in = x0.shape[0]
+    p = 1
+    local_out = point(z_new, oldest * taken_in)
+    while p < vec_out:
+        z_new = jax.lax.ppermute(z_new, axis_name=peer_axis, perm=bank)
+        block_now = point(z_new, (oldest + p) % vec_out * taken_in)
+        local_out = local_out + block_now
+        p = p + 1
+    return local_out
 
 
 def padded_2(array, sides, width):
@@ -144,11 +161,15 @@
     node_pos = lax.axis_index("node")
     tendency = tendency_of(node_states, reaction_matrix, diffusivity)
     own_rows = lax.dynamic_slice_in_dim(weights, node_pos * slots, slots, 0)
-    integral = jnp.einsum(
-        "mj,jtlyx->mtlyx",
-        own_rows,
-        lax.all_gather(tendency, "node", axis=0, tiled=True),
-        precision=lax.Precision.HIGHEST,
+    integral = group_the_levels_all(
+        tendency,
+        "node",
+        lambda part, offset: jnp.einsum(
+            "mj,jtlyx->mtlyx",
+            lax.dynamic_slice_in_dim(own_rows, offset, part.shape[0], axis=1),
+            part,
+            precision=lax.Precision.HIGHEST,
+        ),
     )
     sectioned = initial_state[None] + time_step * integral
     return advect_rows(sectioned, sector_depth, cell_offset, fraction)

time: 330 us -> 306 us (0.927)
  waiting for transfers between devices: 156 us -> 139 us
  between operations: 13.5 us -> 0.14 us
  matrix products: 9.28 us -> 14.2 us
  starting transfers between devices: 7.63 us -> 11 us
    all_gather x1 -> x0, waiting for transfers between devices: 46.7 us -> none  [shards(): lax.all_gather(tendency, 'node', axis=0, tiled=True)]
    ppermute x0 -> x1, waiting for transfers between devices: none -> 30.9 us  [group_the_levels_all(): z_new = jax.lax.ppermute(z_new, axis_name=peer_axis, perm=bank)]
    dot_general x1 -> x2, matrix products: 6.51 us -> 9.02 us  [shards(): jnp.einsum('mj,jtlyx->mtlyx', lax.dynamic_slice_in_dim(own_rows, offset,...]
  transfers between devices with their start and end apart: 6 -> 6, of which waited for: 4 -> 4; matrix products, arithmetic and copies ran while one was open for 1% -> 2% of each run, Pallas kernels for 0% -> 0%
where the time goes in v1:
time: 306 us; the launch traced here: 305 us
  waiting for transfers between devices  139 us (45%)
  local copies, waits for them, and re-layouts  132 us (43%)
  matrix products  14.2 us (5%)
  starting transfers between devices  11 us (4%)
  other arithmetic  8.76 us (3%)
    ppermute x3, waiting for transfers between devices, passed_along(): lax.ppermute(array, axis, [(i, (i + by) % length) for i in range(length)])  108 us
    gather x3, local copies, waits for them, and re-layouts, cut_window(): return lax.dynamic_slice_in_dim(field, start, length, 2)  73.5 us
    transpose x1, local copies, waits for them, and re-layouts, cut_window(): return lax.dynamic_slice_in_dim(field, start, length, 2)  52.8 us
    ppermute x1, waiting for transfers between devices, group_the_levels_all(): z_new = jax.lax.ppermute(z_new, axis_name=peer_axis, perm=bank)  30.9 us
    dot_general x2, matrix products, shards(): jnp.einsum('mj,jtlyx->mtlyx', lax.dynamic_slice_in_dim(own_rows, offset,...  9.02 us
  transfers between devices with their start and end apart: 6, of which 4 were waited for; matrix products, arithmetic and copies ran while one was open for 2% of the time, Pallas kernels for 0%

profile of v1, /device:TPU:0, one launch (start us, length us, event | category | flops | bytes accessed | tf_op | source)
XLA Modules:
  0.0 305.3 jit_solution(13050784915487226809)
XLA Ops:
  0.0 0.0 copy-start
  0.0 2.3 copy.12
  2.3 0.0 copy-start.2
  2.4 1.3 fusion.38
  3.6 1.3 collective-permute-start
  4.9 4.8 %collective-permute-start.1 = (f32[4,8,1,48,128]{4,1,3,2,0:T(8,128)}, f32[4,8,1,48,128]{4,1,3,2,0:T(8,128)}, u32[]{:S(2)}, u32[]{:S(2)}) collective-permute-start(f32[4,8,1,48,128]{4,1,3,2,0:T(8,128)} %get-tuple-element.9), channel_id=1, source_target_pairs={{0,1},{2,3},{4,5},{6,7},{8,9},{10,11},{12,13},{14,15},{16,17},{18,... | collective-permute-start | bytes 2359304 | tf_op jit(solution)/shard_map/ppermute | solution.py:45
  9.7 0.0 copy-done.2
  9.7 1.4 tanh.3
  11.1 0.0 collective-permute-done
  11.1 0.0 collective-permute-done.1
  11.1 1.5 broadcast_select_fusion
  12.6 0.0 copy-done
  12.6 0.1 copy-done.3
  12.7 0.0 copy-done.8
  12.7 4.8 %fusion.5 = f32[4,8,2,48,128]{4,1,3,2,0:T(8,128)S(1)} fusion(f32[4,8,1,48,128]{4,1,3,2,0:T(8,128)S(1)} %get-tuple-element.8, f32[4,8,1,48,128]{4,1,3,2,0:T(8,128)} %get-tuple-element.9, f32[4,8,1,48,128]{4,1,3,2,0:T(8,128)} %get-tuple-element.10, f32[4,8,1,48,128]{4,1,3,2,0:T(8,128)S(1)} %get-tuple-element.7, f32[4,8,2,48,128]{4,3,2,1,0:T(8,128)S(1)} %copy-done.3, ...), kind=kOutput, calls=%fused_computation.12 | convolution fusion | flops 40501248 | bytes 7864584 | tf_op jit(solution)/shard_map/ts,mslyx->mtlyx/dot_general | solution.py:109
  17.5 3.0 collective-permute-start.2
  20.5 0.0 copy-done.9
  20.5 0.0 copy-done.10
  20.5 0.2 fusion.16
  20.7 0.2 fusion.15
  20.9 3.6 %fusion.8 = f32[4,8,2,48,128]{4,0,3,2,1:T(4,128)S(1)} fusion(f32[4,8,2,48,128]{4,1,3,2,0:T(8,128)S(1)} %fusion.5, f32[8,8]{1,0:T(8,128)S(1)} %fusion.15, s32[]{:T(128)S(6)} %select_n.58), kind=kOutput, calls=%fused_computation.15 | convolution fusion | flops 18874368 | bytes 3147780 | tf_op jit(solution)/shard_map/mj,jtlyx->mtlyx/dot_general | solution.py:167
  24.4 0.0 copy-start.7
  24.5 0.0 copy-start.6
  24.5 0.0 copy-start.5
  24.5 30.9 %collective-permute-done.2 = f32[4,8,2,48,128]{4,1,3,2,0:T(8,128)} collective-permute-done((f32[4,8,2,48,128]{4,1,3,2,0:T(8,128)S(1)}, f32[4,8,2,48,128]{4,1,3,2,0:T(8,128)}, u32[]{:S(2)}, u32[]{:S(2)}) %collective-permute-start.2) | collective-permute-done | bytes 1572896 | tf_op jit(solution)/shard_map/ppermute | solution.py:31
  55.3 0.0 copy-done.4
  55.3 5.5 %multiply_add_fusion = f32[4,8,2,48,128]{4,0,3,2,1:T(4,128)S(1)} fusion(f32[4,8,2,48,128]{4,0,3,2,1:T(4,128)S(1)} %fusion.8, f32[8,2,48,128]{3,2,1,0:T(8,128)S(1)} %copy-done.4, f32[4,8,2,48,128]{4,1,3,2,0:T(8,128)} %collective-permute-done.2, f32[8,8]{1,0:T(8,128)S(1)} %fusion.15, s32[]{:T(128)S(6)} %select_n.58, s32[]{:T(128)S(6)} %select_n.65), kind=kOutput, calls=%fused_computation.21 | convolution fusion | flops 20054016 | bytes 5113864 | tf_op jit(solution)/shard_map/mj,jtlyx->mtlyx/dot_general | solution.py:167
  60.8 1.9 collective-permute-start.3
  62.7 35.9 %collective-permute-done.3 = f32[4,8,2,48,128]{4,0,3,2,1:T(4,128)S(1)} collective-permute-done((f32[4,8,2,48,128]{4,0,3,2,1:T(4,128)S(1)}, f32[4,8,2,48,128]{4,0,3,2,1:T(4,128)S(1)}, u32[]{:S(2)}, u32[]{:S(2)}) %collective-permute-start.3) | collective-permute-done | bytes 1572896 | tf_op jit(solution)/shard_map/ppermute | solution.py:53
  98.6 0.0 collective-permute-start.4
  98.6 36.9 %collective-permute-done.4 = f32[4,8,2,48,128]{4,0,3,2,1:T(4,128)} collective-permute-done((f32[4,8,2,48,128]{4,0,3,2,1:T(4,128)S(1)}, f32[4,8,2,48,128]{4,0,3,2,1:T(4,128)}, u32[]{:S(2)}, u32[]{:S(2)}) %collective-permute-start.4) | collective-permute-done | bytes 1572896 | tf_op jit(solution)/shard_map/ppermute | solution.py:53
  135.6 0.0 collective-permute-start.5
  135.6 0.1 copy.10
  135.7 0.1 copy.17
  135.8 0.1 copy.18
  135.9 0.1 copy.19
  136.0 0.1 copy.20
  136.1 0.1 copy.21
  136.2 0.1 copy.22
  136.4 0.1 reshape.22
  136.5 35.3 %collective-permute-done.5 = f32[4,8,2,48,128]{4,0,3,2,1:T(4,128)} collective-permute-done((f32[4,8,2,48,128]{4,0,3,2,1:T(4,128)}, f32[4,8,2,48,128]{4,0,3,2,1:T(4,128)}, u32[]{:S(2)}, u32[]{:S(2)}) %collective-permute-start.5) | collective-permute-done | bytes 1572896 | tf_op jit(solution)/shard_map/ppermute | solution.py:53
  171.8 3.9 %select_add_fusion.1 = (f32[4,8,2,48,128]{4,0,3,2,1:T(4,128)S(1)}, f32[4,8,2,48,128]{4,0,3,2,1:T(4,128)S(1)}) fusion(f32[4,8,2,48,128]{4,0,3,2,1:T(4,128)} %collective-permute-done.5, f32[4,8,2,48,128]{4,0,3,2,1:T(4,128)} %collective-permute-done.4, f32[4,8,2,48,128]{4,0,3,2,1:T(4,128)S(1)} %collective-permute-done.3, pred[4,48]{0,1:T(8,128)(4,1)S(1)} %copy.18, ...), kind=kLoop, calls=%fused_computation.20 | loop fusion | flops 4718592 | bytes 9438528 | tf_op jit(solution)/shard_map/add | solution.py:131
  175.7 0.8 maximum_bitcast_fusion
  176.5 52.8 %copy.23 = f32[4,48,8,2,256]{2,3,1,0,4:T(2,128)} copy(f32[4,48,8,2,256]{4,0,1,3,2:T(4,128)S(1)} %maximum_bitcast_fusion) | data formatting | bytes 6291456 | tf_op jit(solution)/shard_map/vmap(vmap())/transpose | solution.py:116
  229.2 36.2 %gather_fusion = f32[192,8,2,131]{1,2,3,0:T(2,128)} fusion(f32[4,48,8,2,256]{2,3,1,0,4:T(2,128)} %copy.23, s32[192]{0:T(256)S(1)} %reshape.22), kind=kCustom, calls=%fused_computation | custom fusion | bytes 3223296 | tf_op jit(solution)/shard_map/vmap(vmap())/gather | solution.py:116
  265.5 37.2 %copy.24 = f32[4,48,8,2,131]{4,1,3,2,0:T(8,128)S(1)} copy(f32[4,48,8,2,131]{2,3,4,1,0:T(2,128)} %bitcast.31) | data formatting | bytes 3219456 | tf_op jit(solution)/shard_map/vmap(vmap())/gather | solution.py:116
  302.7 0.0 copy-start.1
  302.7 2.5 fusion
  (12 shorter events, 0.0 us)
Async XLA Ops:
  0.0 12.6 %copy-start = (f32[8,8]{1,0:T(8,128)S(1)}, f32[8,8]{1,0:T(8,128)}, u32[]{:S(2)}) copy-start(f32[8,8]{1,0:T(8,128)} %param.15) | copy-start | bytes 772
  2.3 7.4 %copy-start.2 = (f32[4,8,2,48,128]{4,3,2,1,0:T(8,128)S(1)}, f32[4,8,2,48,128]{4,3,2,1,0:T(8,128)}, u32[]{:S(2)}) copy-start(f32[4,8,2,48,128]{4,3,2,1,0:T(8,128)} %param.10) | copy-start | bytes 4718596
  3.6 7.4 %collective-permute-start = (f32[4,8,1,48,128]{4,1,3,2,0:T(8,128)}, f32[4,8,1,48,128]{4,1,3,2,0:T(8,128)}, u32[]{:S(2)}, u32[]{:S(2)}) collective-permute-start(f32[4,8,1,48,128]{4,1,3,2,0:T(8,128)} %get-tuple-element.10), channel_id=1, source_target_pairs={{1,0},{3,2},{5,4},{7,6},{9,8},{11,10},{13,12},{15,14},{17,16},{19,... | collective-permute-start | bytes 2359304 | tf_op jit(solution)/shard_map/ppermute | solution.py:46
  4.9 6.2 %collective-permute-start.1 = (f32[4,8,1,48,128]{4,1,3,2,0:T(8,128)}, f32[4,8,1,48,128]{4,1,3,2,0:T(8,128)}, u32[]{:S(2)}, u32[]{:S(2)}) collective-permute-start(f32[4,8,1,48,128]{4,1,3,2,0:T(8,128)} %get-tuple-element.9), channel_id=1, source_target_pairs={{0,1},{2,3},{4,5},{6,7},{8,9},{10,11},{12,13},{14,15},{16,17},{18,... | collective-permute-start | bytes 2359304 | tf_op jit(solution)/shard_map/ppermute | solution.py:45
  11.1 1.6 copy-start.3
  11.1 1.6 copy-start.8
  12.7 7.8 %copy-start.9 = (s32[8]{0:T(128)S(1)}, s32[8]{0:T(128)}, u32[]{:S(2)}) copy-start(s32[8]{0:T(128)} %param.11) | copy-start | bytes 100
  12.7 7.8 %copy-start.10 = (f32[8,8]{1,0:T(8,128)S(1)}, f32[8,8]{1,0:T(8,128)}, u32[]{:S(2)}) copy-start(f32[8,8]{1,0:T(8,128)} %constant.81.clone) | copy-start | bytes 772
  17.5 37.8 %collective-permute-start.2 = (f32[4,8,2,48,128]{4,1,3,2,0:T(8,128)S(1)}, f32[4,8,2,48,128]{4,1,3,2,0:T(8,128)}, u32[]{:S(2)}, u32[]{:S(2)}) collective-permute-start(f32[4,8,2,48,128]{4,1,3,2,0:T(8,128)S(1)} %fusion.5), channel_id=1, source_target_pairs={{0,2},{2,0},{1,3},{3,1},{4,6},{6,4},{5,7},{7,5},{8,10},{10,8},{9,1... | collective-permute-start | bytes 4718600 | tf_op jit(solution)/shard_map/ppermute | solution.py:31
  20.9 34.5 %copy-start.4 = (f32[8,2,48,128]{3,2,1,0:T(8,128)S(1)}, f32[8,2,48,128]{3,2,1,0:T(8,128)}, u32[]{:S(2)}) copy-start(f32[8,2,48,128]{3,2,1,0:T(8,128)} %param.9) | copy-start | bytes 1179652
  24.4 111.1 %copy-start.7 = (s32[4,48]{1,0:T(4,128)S(1)}, s32[4,48]{1,0:T(4,128)}, u32[]{:S(2)}) copy-start(s32[4,48]{1,0:T(4,128)} %param.12) | copy-start | bytes 2308
  24.5 111.9 %copy-start.6 = (s32[4,48]{1,0:T(4,128)S(1)}, s32[4,48]{1,0:T(4,128)}, u32[]{:S(2)}) copy-start(s32[4,48]{1,0:T(4,128)} %param.13) | copy-start | bytes 2308
  24.5 112.0 %copy-start.5 = (f32[4,48]{1,0:T(4,128)S(1)}, f32[4,48]{1,0:T(4,128)}, u32[]{:S(2)}) copy-start(f32[4,48]{1,0:T(4,128)} %param.14) | copy-start | bytes 2308
  60.8 37.8 %collective-permute-start.3 = (f32[4,8,2,48,128]{4,0,3,2,1:T(4,128)S(1)}, f32[4,8,2,48,128]{4,0,3,2,1:T(4,128)S(1)}, u32[]{:S(2)}, u32[]{:S(2)}) collective-permute-start(f32[4,8,2,48,128]{4,0,3,2,1:T(4,128)S(1)} %multiply_add_fusion), channel_id=1, source_target_pairs={{0,4},{4,8},{8,12},{12,0},{1,5},{5,9},{9,13},{13,1},{2,6},{6,10},{... | collective-permute-start | bytes 4718600 | tf_op jit(solution)/shard_map/ppermute | solution.py:53
  98.6 36.9 %collective-permute-start.4 = (f32[4,8,2,48,128]{4,0,3,2,1:T(4,128)S(1)}, f32[4,8,2,48,128]{4,0,3,2,1:T(4,128)}, u32[]{:S(2)}, u32[]{:S(2)}) collective-permute-start(f32[4,8,2,48,128]{4,0,3,2,1:T(4,128)S(1)} %collective-permute-done.3), channel_id=1, source_target_pairs={{0,4},{4,8},{8,12},{12,0},{1,5},{5,9},{9,13},{13,1},{2,6},{6,10},{... | collective-permute-start | bytes 4718600 | tf_op jit(solution)/shard_map/ppermute | solution.py:53
  135.6 36.2 %collective-permute-start.5 = (f32[4,8,2,48,128]{4,0,3,2,1:T(4,128)}, f32[4,8,2,48,128]{4,0,3,2,1:T(4,128)}, u32[]{:S(2)}, u32[]{:S(2)}) collective-permute-start(f32[4,8,2,48,128]{4,0,3,2,1:T(4,128)} %collective-permute-done.4), channel_id=1, source_target_pairs={{0,4},{4,8},{8,12},{12,0},{1,5},{5,9},{9,13},{13,1},{2,6},{6,10},{... | collective-permute-start | bytes 4718600 | tf_op jit(solution)/shard_map/ppermute | solution.py:53
  302.7 2.6 copy-start.1
